TPU v7x, 128 devices: a whole 4x4x4 slice. The times are simulated.
128 devices in a mesh: seq: 16 (over x, z), head: 8 (over y, core).
Axes of the slice: x: 4, y: 4, z: 4, core: 2. Of those that a mesh axis runs over, the one named last changes fastest.
Arguments:
- queries: float32 [4096, 8192], P('seq', 'head'), may hold values from -8 to 8
- key_heads: float32 [4096, 1024], P('seq', 'head'), may hold values from -6 to 6
- value_heads: float32 [4096, 1024], P('seq', 'head'), may hold values from -6 to 6
- query_map: float32 [64, 128, 128], P('head'), may hold values from -0.5 to 0.5
- key_map: float32 [8, 128, 128], P('head'), may hold values from -0.5 to 0.5
Outputs:
- query_map_step: float32 [64, 128, 128], P('head')
- key_map_step: float32 [8, 128, 128], P('head')
All inputs are finite; a program needn't handle non-finite values.
Results may differ from a plain program's by a relative error of at most 0.00019.
Values sent between devices are 32-bit elements; how exact they have to be, the bound alone decides.
A program may use at most 64 MiB of HBM per device.

v0:
```python
import math

import jax
import jax.numpy as jnp
from jax import lax
from jax.experimental import pallas as pl
from jax.experimental.pallas import tpu as pltpu
from jax.sharding import PartitionSpec as P

NEGATIVE = -1e30
EPSILON = 1e-06
F32 = jnp.float32
BF16 = jnp.bfloat16


def halves(x):
    hi = x.astype(BF16)
    return hi, (x - hi.astype(F32)).astype(BF16)


def pair(x):
    return jnp.concatenate(halves(x), axis=1)


def twice(x, axis):
    return jnp.concatenate([x, x], axis=axis)


def stacked(x):
    hi, lo = halves(x)
    return jnp.concatenate([hi, hi, lo, lo], axis=0)


def dot(a, b):
    return jnp.dot(a, b, preferred_element_type=F32)


def dot_rows(a, b):
    return lax.dot_general(a, b, (((0,), (0,)), ((), ())), preferred_element_type=F32)


def fold(x):
    w = x.shape[1] // 2
    return x[:, :w] + x[:, w:]


def quad(x):
    h = x.shape[0] // 2
    y = fold(x)
    return y[:h] + y[h:]


def softplus_and_slope(x):
    e = jnp.exp(-jnp.abs(x))
    soft = jnp.maximum(x, 0.0) + jnp.log1p(e)
    slope = jnp.where(x >= 0.0, 1.0, e) / (1.0 + e)
    return soft, slope


MESH = pl.DeviceIdType.MESH


class Messages:
    def __init__(self, send_sems, recv_sems):
        self.send_sems, self.recv_sems, self.all = send_sems, recv_sems, {}

    def make(self, name, ref, peer):
        at = len(self.all)
        self.all[name] = pltpu.make_async_remote_copy(
            src_ref=ref, dst_ref=ref, send_sem=self.send_sems.at[at], recv_sem=self.recv_sems.at[at],
            device_id={"seq": peer}, device_id_type=MESH,
        )

    def start(self, *names):
        for name in names:
            self.all[name].start()

    def arrived(self, *names):
        for name in names:
            self.all[name].wait_recv()

    def sent(self):
        for copy in self.all.values():
            copy.wait_send()


def kernel(q_ref, k_ref, v_ref, qmap_ref, kmap_ref, gq_ref, gk_ref,
           q4, k4t, v4, sgk, sstate, norm, acc, top, tot, num, den, feat, a4, sgq,
           kbuf, vbuf, grad, parts, mine, whole, squares, head_squares, seq_squares,
           kv_send, kv_recv, rs_send, rs_recv, ag_send, ag_recv, sq_send, sq_recv):
    heads, dh = qmap_ref.shape[0], qmap_ref.shape[1]
    tok = q_ref.shape[0]
    me = lax.axis_index("seq")
    my_head = lax.axis_index("head")
    n_seq, n_head = kbuf.shape[0], head_squares.shape[0] + 1
    side = math.isqrt(n_seq)
    my_x, my_z = me // side, lax.rem(me, side)

    def at(dx, dz):
        return lax.rem(my_x + dx + side, side) * side + lax.rem(my_z + dz + side, side)

    barrier = pltpu.get_barrier_semaphore()

    def greet_seq(k, _):
        pl.semaphore_signal(barrier, inc=1, device_id={"seq": lax.rem(me + k, n_seq)}, device_id_type=MESH)
        return 0

    def greet_head(k, _):
        pl.semaphore_signal(barrier, inc=1, device_id={"head": lax.rem(my_head + k, n_head)}, device_id_type=MESH)
        return 0

    lax.fori_loop(1, n_seq, greet_seq, 0)
    lax.fori_loop(1, n_head, greet_head, 0)
    kbuf[me] = k_ref[...]
    vbuf[me] = v_ref[...]
    pl.semaphore_wait(barrier, n_seq + n_head - 2)

    half = tok // 2
    msgs = Messages(kv_send, kv_recv)
    for tag, buf, flip in (("k", kbuf, False), ("v", vbuf, True)):
        def place(a, b):
            return at(b, a) if flip else at(a, b)

        def route(name, a, b, first):
            up = place(1, 0) if first else place(0, 1)
            down = place(-1, 0) if first else place(0, -1)
            msgs.make(tag + name + "+", buf.at[place(a, b)], up)
            msgs.make(tag + name + "-", buf.at[place(a, b)], down)
            pa, pb, na, nb = (a - 1, b, a + 1, b) if first else (a, b - 1, a, b + 1)
            msgs.make(tag + name + "++", buf.at[place(pa, pb), pl.ds(0, half)], up)
            msgs.make(tag + name + "--", buf.at[place(na, nb), pl.ds(half, half)], down)

        route("1", 0, 0, True)
        for name, a in (("a", 0), ("b", -1), ("c", 1), ("d", 2)):
            route(name, a, 0, False)

    def both(*names):
        return [t + x for t in "kv" for x in names]

    scale = dh ** -0.5 * math.log2(math.e)
    rows = lax.broadcasted_iota(jnp.int32, (tok, tok), 0)
    cols = lax.broadcasted_iota(jnp.int32, (tok, tok), 1)
    causal = rows >= cols
    kmap2 = twice(pair(kmap_ref[0]), 0)

    def prepare(j):
        k, v = kbuf[j], vbuf[j]
        k4t[j] = stacked(k.T * scale)
        v2 = pair(v)
        v4[j] = twice(v2, 0)
        act = fold(dot(pair(k), kmap2))
        b, slope = softplus_and_slope(act)
        sgk[j] = slope
        return b, v2

    def prefix(j, _):
        b, v2 = prepare(j)
        sstate[...] += quad(dot_rows(pair(b), v2))
        norm[...] += jnp.sum(b, axis=0, keepdims=True)
        return 0

    def attend(h, j, first):
        s = dot(q4[h], k4t[j])
        if first:
            s = jnp.where(causal, s, NEGATIVE)
        new = jnp.max(s, axis=1, keepdims=True)
        if first:
            new = jnp.broadcast_to(new, (tok, dh))
        else:
            old = top[h]
            new = jnp.maximum(old, new)
            alpha = jnp.exp2(old - new)
        p = jnp.exp2(s - twice(new, 1))
        o = fold(dot(pair(p), v4[j]))
        if first:
            tot[h] = fold(p)
            acc[h] = o
        else:
            tot[h] = tot[h] * alpha + fold(p)
            acc[h] = acc[h] * alpha + o
        top[h] = new

    msgs.start(*both("1+", "1-", "a+", "a-"))
    sstate[...] = jnp.zeros_like(sstate)
    norm[...] = jnp.zeros_like(norm)
    b_own, v2_own = prepare(me)
    v_own = v_ref[...]
    b4 = twice(pair(b_own), 0)
    b4t = stacked(b_own.T)
    v4t = stacked(v_own.T)

    def before(h, _):
        q2 = pair(q_ref[:, pl.ds(pl.multiple_of(h * dh, dh), dh)])
        q4[h] = twice(q2, 1)
        act = fold(dot(q2, twice(pair(qmap_ref[h]), 0)))
        a, slope = softplus_and_slope(act)
        sgq[h] = slope
        feat[h] = a
        a4[h] = twice(pair(a), 1)
        ker = jnp.where(causal, dot(a4[h], b4t), 0.0)
        den[h] = jnp.broadcast_to(jnp.sum(ker, axis=1, keepdims=True), (tok, dh))
        num[h] = fold(dot(pair(ker), v4[me]))
        attend(h, me, True)
        return 0

    lax.fori_loop(0, heads, before, 0)

    def block(j):
        @pl.when(j < me)
        def _():
            prefix(j, 0)

            def two(h, _):
                attend(2 * h, j, False)
                attend(2 * h + 1, j, False)
                return 0

            lax.fori_loop(0, heads // 2, two, 0)

    def near(t, _):
        step = 2 * lax.rem(t, 2) - 1
        block(at(step * (1 - t // 2), step * (t // 2)))
        return 0

    def across(t, _):
        block(at(2 * t, 2 * (1 - t)))
        return 0

    def corner(t, _):
        block(at(2 * (t // 2) - 1, 2 * lax.rem(t, 2) - 1))
        return 0

    def knight(t, _):
        step = 2 * lax.rem(t, 2) - 1
        block(at(step * (1 - t // 2) + 2 * (t // 2), 2 * (1 - t // 2) + step * (t // 2)))
        return 0

    msgs.arrived(*both("1+", "1-"))
    msgs.start(*both("1++", "1--", "b+", "b-", "c+", "c-"))
    msgs.arrived(*both("a+", "a-"))
    msgs.start(*both("a++", "a--"))
    lax.fori_loop(0, 4, near, 0)
    msgs.arrived(*both("1++", "1--"))
    msgs.start(*both("d+", "d-"))
    msgs.arrived(*both("a++", "a--"))
    lax.fori_loop(0, 2, across, 0)
    msgs.arrived(*both("b+", "b-", "c+", "c-"))
    msgs.start(*both("b++", "b--", "c++", "c--"))
    lax.fori_loop(0, 4, corner, 0)
    msgs.arrived(*both("d+", "d-"))
    msgs.start(*both("d++", "d--"))
    msgs.arrived(*both("b++", "b--", "c++", "c--"))
    lax.fori_loop(0, 4, knight, 0)
    msgs.arrived(*both("d++", "d--"))
    block(at(2, 2))

    state2 = twice(pair(sstate[...]), 0)
    state2t = twice(pair(sstate[...].T), 0)
    norm_row = norm[...]

    def after(h, carry):
        adj, adjn, gkd = carry
        a = feat[h]
        a2 = a4[h, :, : 2 * dh]
        q2 = q4[h, :, : 2 * dh]
        rden = 1.0 / (den[h] + jnp.sum(a * norm_row, axis=1, keepdims=True))
        student = (num[h] + fold(dot(a2, state2))) * rden
        teacher = acc[h] / jnp.sum(tot[h], axis=1, keepdims=True)
        mis = student - teacher
        gn = mis * rden
        gd = -jnp.sum(gn * student, axis=1, keepdims=True)
        gn2 = pair(gn)
        coup = jnp.where(causal, dot(twice(gn2, 1), v4t) + gd, 0.0)
        c2 = pair(coup)
        gq = fold(dot(c2, b4)) + fold(dot(gn2, state2t)) + gd * norm_row
        grad[h] = quad(dot_rows(q2, pair(gq * sgq[h])))
        adj = adj + quad(dot_rows(a2, gn2))
        adjn = adjn + jnp.sum(a * gd, axis=0, keepdims=True)
        gkd = gkd + quad(dot_rows(c2, a2))
        return adj, adjn, gkd

    width = dh // n_seq
    groups = ((0, heads // 2), (heads // 2, heads // 2), (heads, 1))

    def rows_of(d):
        return pl.ds(pl.multiple_of(d * width, width), width)

    def scatter(g):
        first, count = groups[g]

        def send(k, _):
            peer = lax.rem(me + k, n_seq)
            pltpu.make_async_remote_copy(
                src_ref=grad.at[pl.ds(first, count), rows_of(peer)],
                dst_ref=parts.at[k - 1, pl.ds(first, count)],
                send_sem=rs_send.at[g], recv_sem=rs_recv.at[g],
                device_id={"seq": peer}, device_id_type=MESH,
            ).start()
            return 0

        lax.fori_loop(1, n_seq, send, 0)

    def all_of(ref, sem):
        pltpu.make_async_copy(ref, ref, sem).wait()

    def gather(g):
        first, count = groups[g]
        span = pl.ds(first, count)
        all_of(parts.at[:, span], rs_recv.at[g])
        total = grad[span, rows_of(me)]
        for k in range(n_seq - 1):
            total = total + parts[k, span]
        mine[span] = total
        whole[span, rows_of(me)] = total

        def send(k, _):
            pltpu.make_async_remote_copy(
                src_ref=mine.at[span],
                dst_ref=whole.at[span, rows_of(me)],
                send_sem=ag_send.at[g], recv_sem=ag_recv.at[g],
                device_id={"seq": lax.rem(me + k, n_seq)}, device_id_type=MESH,
            ).start()
            return 0

        lax.fori_loop(1, n_seq, send, 0)
        return jnp.sum(total * total, axis=0)

    carry = (jnp.zeros((dh, dh), F32), jnp.zeros((1, dh), F32), jnp.zeros((tok, dh), F32))
    carry = lax.fori_loop(0, heads // 2, after, carry)
    scatter(0)
    adj, adjn, gkd = lax.fori_loop(heads // 2, heads, after, carry)
    scatter(1)
    adjt2 = twice(pair(adj.T), 0)

    grad[heads] = quad(dot_rows(pair(k_ref[...]), pair(gkd * sgk[me])))

    def later(j, _):
        g = fold(dot(v4[j, :tok], adjt2)) + adjn
        grad[heads] += quad(dot_rows(pair(kbuf[j]), pair(g * sgk[j])))
        return 0

    lax.fori_loop(0, me, later, 0)
    scatter(2)
    squares[0] = gather(0) + gather(1) + gather(2)

    def send_head(k, _):
        pltpu.make_async_remote_copy(
            src_ref=squares.at[0], dst_ref=head_squares.at[k - 1],
            send_sem=sq_send.at[0], recv_sem=sq_recv.at[0],
            device_id={"head": lax.rem(my_head + k, n_head)}, device_id_type=MESH,
        ).start()
        return 0

    def send_seq(k, _):
        pltpu.make_async_remote_copy(
            src_ref=squares.at[1], dst_ref=seq_squares.at[k - 1],
            send_sem=sq_send.at[1], recv_sem=sq_recv.at[1],
            device_id={"seq": lax.rem(me + k, n_seq)}, device_id_type=MESH,
        ).start()
        return 0

    lax.fori_loop(1, n_head, send_head, 0)
    all_of(head_squares, sq_recv.at[0])
    squares[1] = squares[0] + jnp.sum(head_squares[...], axis=0)
    lax.fori_loop(1, n_seq, send_seq, 0)
    all_of(seq_squares, sq_recv.at[1])
    square = jnp.sum(squares[1] + jnp.sum(seq_squares[...], axis=0))
    size = (heads + 1) * n_head * dh * grad.shape[2]
    factor = 1.0 / jnp.sqrt(jnp.broadcast_to(square / size + EPSILON, (1, dh)))
    for g in range(3):
        first, count = groups[g]
        all_of(parts.at[:, pl.ds(first, count)], ag_recv.at[g])
    gq_ref[...] = whole[pl.ds(0, heads)] * factor
    gk_ref[...] = whole[pl.ds(heads, 1)] * factor

    msgs.sent()
    for g in range(3):
        first, count = groups[g]
        all_of(parts.at[:, pl.ds(first, count)], rs_send.at[g])
        all_of(parts.at[:, pl.ds(first, count)], ag_send.at[g])
    all_of(head_squares, sq_send.at[0])
    all_of(seq_squares, sq_send.at[1])


def on_device(queries, key_heads, value_heads, query_map, key_map):
    tok = queries.shape[0]
    heads, dh, feats = query_map.shape
    n = lax.axis_size("seq")
    return pl.pallas_call(
        kernel,
        out_shape=(jax.ShapeDtypeStruct((heads, dh, feats), F32), jax.ShapeDtypeStruct((1, dh, feats), F32)),
        in_specs=[pl.BlockSpec(memory_space=pltpu.VMEM)] * 5,
        out_specs=(pl.BlockSpec(memory_space=pltpu.VMEM),) * 2,
        scratch_shapes=[
            pltpu.VMEM((heads, tok, 4 * dh), BF16),
            pltpu.VMEM((n, 4 * dh, tok), BF16),
            pltpu.VMEM((n, 2 * tok, 2 * dh), BF16),
            pltpu.VMEM((n, tok, feats), F32),
            pltpu.VMEM((feats, dh), F32),
            pltpu.VMEM((1, feats), F32),
            pltpu.VMEM((heads, tok, dh), F32),
            pltpu.VMEM((heads, tok, dh), F32),
            pltpu.VMEM((heads, tok, dh), F32),
            pltpu.VMEM((heads, tok, dh), F32),
            pltpu.VMEM((heads, tok, dh), F32),
            pltpu.VMEM((heads, tok, feats), F32),
            pltpu.VMEM((heads, tok, 4 * feats), BF16),
            pltpu.VMEM((heads, tok, feats), F32),
            pltpu.VMEM((n, tok, dh), F32),
            pltpu.VMEM((n, tok, dh), F32),
            pltpu.VMEM((heads + 1, dh, feats), F32),
            pltpu.VMEM((n - 1, heads + 1, dh // n, feats), F32),
            pltpu.VMEM((heads + 1, dh // n, feats), F32),
            pltpu.VMEM((heads + 1, dh, feats), F32),
            pltpu.VMEM((2, dh // n, feats), F32),
            pltpu.VMEM((lax.axis_size("head") - 1, dh // n, feats), F32),
            pltpu.VMEM((n - 1, dh // n, feats), F32),
            pltpu.SemaphoreType.DMA((40,)),
            pltpu.SemaphoreType.DMA((40,)),
        ] + [pltpu.SemaphoreType.DMA((3,))] * 4 + [pltpu.SemaphoreType.DMA((2,))] * 2,
        compiler_params=pltpu.CompilerParams(vmem_limit_bytes=56 * 2**20, collective_id=0, has_side_effects=True),
    )(queries, key_heads, value_heads, query_map, key_map)


def solution(mesh):
    return jax.shard_map(
        on_device,
        mesh=mesh,
        in_specs=(P("seq", "head"), P("seq", "head"), P("seq", "head"), P("head"), P("head")),
        out_specs=(P("head"), P("head")),
        check_vma=False,
    )
```

profile of v0, /device:TPU:1, one launch (start us, length us, event | category | flops | bytes accessed | tf_op | source)
XLA Modules:
  0.0 98.7 jit_solution(9337583446418117030)
XLA Ops:
  0.6 95.5 %shard_map.68 = (f32[8,128,128]{2,1,0:T(8,128)}, f32[1,128,128]{2,1,0:T(8,128)}) custom-call(f32[256,1024]{1,0:T(8,128)} %q_ref.1, f32[256,128]{1,0:T(8,128)} %k_ref.1, f32[256,128]{1,0:T(8,128)} %v_ref.1, f32[8,128,128]{2,1,0:T(8,128)} %qmap_ref.1, f32[1,128,128]{2,1,0:T(8,128)} %kmap_ref.1), custom_call_target="tpu_custom_call" | custom-call | tf_op jit(solution)/shard_map/pallas_call | solution.py:389
  96.1 0.0 copy-start
  96.1 1.9 %copy.9 = f32[8,128,128]{2,1,0:T(8,128)} copy(f32[8,128,128]{2,1,0:T(8,128)} %get-tuple-element.4) | data formatting | bytes 1048576
  98.0 0.0 copy-done
  98.0 0.6 copy.10
Async XLA Ops:
  96.1 1.9 %copy-start = (f32[1,128,128]{2,1,0:T(8,128)S(1)}, f32[1,128,128]{2,1,0:T(8,128)}, u32[]{:S(2)}) copy-start(f32[1,128,128]{2,1,0:T(8,128)} %get-tuple-element.5) | copy-start | bytes 196612
where the time goes:
time: 98.8 us; the launch traced here: 98.7 us
  Pallas kernels  95.5 us (97%)
  local copies, waits for them, and re-layouts  2.54 us (3%)
    pallas_call x1, Pallas kernels, on_device(): pl.pallas_call(kernel, out_shape=(jax.ShapeDtypeStruct((heads, dh, feats)...  95.5 us
    unnamed x4, local copies, waits for them, and re-layouts  2.54 us

commit v1 on v0

v1 whole, which is shorter than its diff:
```python
import math

import jax
import jax.numpy as jnp
from jax import lax
from jax.experimental import pallas as pl
from jax.experimental.pallas import tpu as pltpu
from jax.sharding import PartitionSpec as P

NEGATIVE = -1e30
EPSILON = 1e-06
F32 = jnp.float32
BF16 = jnp.bfloat16


def halves(x):
    hi = x.astype(BF16)
    return hi, (x - hi.astype(F32)).astype(BF16)


def pair(x):
    return jnp.concatenate(halves(x), axis=1)


def twice(x, axis):
    return jnp.concatenate([x, x], axis=axis)


def stacked(x):
    hi, lo = halves(x)
    return jnp.concatenate([hi, hi, lo, lo], axis=0)


def dot(a, b):
    return jnp.dot(a, b, preferred_element_type=F32)


def dot_rows(a, b):
    return lax.dot_general(a, b, (((0,), (0,)), ((), ())), preferred_element_type=F32)


def fold(x):
    w = x.shape[1] // 2
    return x[:, :w] + x[:, w:]


def quad(x):
    h = x.shape[0] // 2
    y = fold(x)
    return y[:h] + y[h:]


def softplus_and_slope(x):
    e = jnp.exp(-jnp.abs(x))
    soft = jnp.maximum(x, 0.0) + jnp.log1p(e)
    slope = jnp.where(x >= 0.0, 1.0, e) / (1.0 + e)
    return soft, slope


MESH = pl.DeviceIdType.MESH


class Messages:
    def __init__(self, send_sems, recv_sems):
        self.send_sems, self.recv_sems, self.all = send_sems, recv_sems, {}

    def make(self, name, ref, peer):
        at = len(self.all)
        self.all[name] = pltpu.make_async_remote_copy(
            src_ref=ref, dst_ref=ref, send_sem=self.send_sems.at[at], recv_sem=self.recv_sems.at[at],
            device_id={"seq": peer}, device_id_type=MESH,
        )

    def start(self, *names):
        for name in names:
            self.all[name].start()

    def arrived(self, *names):
        for name in names:
            self.all[name].wait_recv()

    def sent(self):
        for copy in self.all.values():
            copy.wait_send()


def kernel(q_ref, k_ref, v_ref, qmap_ref, kmap_ref, gq_ref, gk_ref,
           q4, k4t, v4, k2t, sgk, state, norm, acc, top, tot, num, den, feat, a4, sgq, b4, b4t, v4t, adjs, adjt2, adjns, gkds,
           kbuf, vbuf, qbuf, grad, parts, mine, whole, squares, head_squares, seq_squares,
           kv_send, kv_recv, q_send, q_recv, rs_send, rs_recv, ag_send, ag_recv, sq_send, sq_recv):
    heads, dh = qmap_ref.shape[0], qmap_ref.shape[1]
    tok = q_ref.shape[0]
    me = lax.axis_index("seq")
    my_head = lax.axis_index("head")
    n_seq, n_head = kbuf.shape[0], head_squares.shape[0] + 1
    side = math.isqrt(n_seq)
    my_x, my_z = me // side, lax.rem(me, side)
    given = qbuf.shape[1] // dh
    kept = heads - given
    far = n_seq - 1 - me
    early = me < n_seq // 2
    main = list(range(kept))
    rest = list(range(kept, heads))
    guest = list(range(heads, heads + given))

    def at(dx, dz):
        return lax.rem(my_x + dx + side, side) * side + lax.rem(my_z + dz + side, side)

    barrier = pltpu.get_barrier_semaphore()
    for peer in (at(1, 0), at(-1, 0), at(0, 1), at(0, -1), far):
        pl.semaphore_signal(barrier, inc=1, device_id={"seq": peer}, device_id_type=MESH)

    def greet_head(k, _):
        pl.semaphore_signal(barrier, inc=1, device_id={"head": lax.rem(my_head + k, n_head)}, device_id_type=MESH)
        return 0

    lax.fori_loop(1, n_head, greet_head, 0)
    kbuf[me] = k_ref[...]
    vbuf[me] = v_ref[...]

    half = tok // 2
    msgs = Messages(kv_send, kv_recv)
    for tag, buf, flip in (("k", kbuf, False), ("v", vbuf, True)):
        def place(a, b):
            return at(b, a) if flip else at(a, b)

        def route(name, a, b, first):
            up = place(1, 0) if first else place(0, 1)
            down = place(-1, 0) if first else place(0, -1)
            msgs.make(tag + name + "+", buf.at[place(a, b)], up)
            msgs.make(tag + name + "-", buf.at[place(a, b)], down)
            pa, pb, na, nb = (a - 1, b, a + 1, b) if first else (a, b - 1, a, b + 1)
            msgs.make(tag + name + "++", buf.at[place(pa, pb), pl.ds(0, half)], up)
            msgs.make(tag + name + "--", buf.at[place(na, nb), pl.ds(half, half)], down)

        route("1", 0, 0, True)
        for name, a in (("a", 0), ("b", -1), ("c", 1), ("d", 2)):
            route(name, a, 0, False)

    def both(*names):
        return [t + x for t in "kv" for x in names]

    query_copy = pltpu.make_async_remote_copy(
        src_ref=q_ref.at[:, pl.ds(kept * dh, given * dh)], dst_ref=qbuf,
        send_sem=q_send.at[0], recv_sem=q_recv.at[0], device_id={"seq": far}, device_id_type=MESH,
    )

    scale = dh ** -0.5 * math.log2(math.e)
    rows = lax.broadcasted_iota(jnp.int32, (tok, tok), 0)
    cols = lax.broadcasted_iota(jnp.int32, (tok, tok), 1)
    causal = rows >= cols
    kmap2 = twice(pair(kmap_ref[0]), 0)

    def prepare(j):
        k, v = kbuf[j], vbuf[j]
        kt = k.T
        keys = stacked(kt * scale)
        k4t[j] = keys
        k2t[j] = jnp.concatenate(halves(kt), axis=0)
        v2 = pair(v)
        values = twice(v2, 0)
        v4[j] = values
        b, slope = softplus_and_slope(fold(dot(pair(k), kmap2)))
        sgk[j] = slope
        return keys, values, b, v2

    def diagonal(n, b, v):
        b4[n] = twice(pair(b), 0)
        b4t[n] = stacked(b.T)
        v4t[n] = stacked(v.T)

    def attend(group, keys, values, masked=False, fresh=False):
        scores = [dot(q4[h], keys) for h in group]
        if not fresh:
            before = [(top[h], tot[h], acc[h]) for h in group]
        found = []
        for i, s in enumerate(scores):
            if masked:
                s = jnp.where(causal, s, NEGATIVE)
            new = jnp.max(s, axis=1, keepdims=True)
            if fresh:
                new = jnp.broadcast_to(new, (tok, dh))
            else:
                new = jnp.maximum(before[i][0], new)
                alpha = jnp.exp2(before[i][0] - new)
            p = jnp.exp2(s - twice(new, 1))
            o = fold(dot(pair(p), values))
            t = fold(p)
            if not fresh:
                t = before[i][1] * alpha + t
                o = before[i][2] * alpha + o
            found.append((new, t, o))
        for h, (new, t, o) in zip(group, found):
            top[h], tot[h], acc[h] = new, t, o

    def load_queries(slots, source):
        for h, q in zip(slots, source):
            q4[h] = twice(pair(q), 1)

    def before(slots, names, n, j, fresh):
        values = v4[j]
        acts = [fold(dot(q4[h, :, : 2 * dh], twice(pair(qmap_ref[m]), 0))) for h, m in zip(slots, names)]
        soft = [softplus_and_slope(act) for act in acts]
        a4s = [twice(pair(a), 1) for a, _ in soft]
        for h, (a, slope), four in zip(slots, soft, a4s):
            feat[h], sgq[h], a4[h] = a, slope, four
        kers = [jnp.where(causal, dot(four, b4t[n]), 0.0) for four in a4s]
        nums = [fold(dot(pair(ker), values)) for ker in kers]
        for h, ker, nm in zip(slots, kers, nums):
            den[h] = jnp.broadcast_to(jnp.sum(ker, axis=1, keepdims=True), (tok, dh))
            num[h] = nm
        attend(slots, k4t[j], values, masked=True, fresh=fresh)

    def own_queries(slots):
        return [q_ref[:, h * dh : (h + 1) * dh] for h in slots]

    state[...] = jnp.zeros_like(state)
    norm[...] = jnp.zeros_like(norm)
    adjns[...] = jnp.zeros_like(adjns)
    adjt2[...] = jnp.zeros_like(adjt2)
    _, _, b_own, v2_own = prepare(me)
    diagonal(0, b_own, v_ref[...])
    state_own = quad(dot_rows(pair(b_own), v2_own))
    norm_own = jnp.sum(b_own, axis=0, keepdims=True)

    def add_state(n, s, b):
        state[n] += s
        norm[n] += b

    def begin(slots):
        load_queries(slots, own_queries(slots))
        before(slots, slots, 0, me, True)

    cut = kept // 2
    begin(main[:cut])
    pl.semaphore_wait(barrier, n_head + 4)
    msgs.start(*both("1+", "1-", "a+", "a-"))

    @pl.when(jnp.logical_not(early))
    def _():
        query_copy.start()

    begin(main[cut:])

    @pl.when(early)
    def _():
        begin(rest)
        add_state(1, state_own, norm_own)

    msgs.arrived(*both("1+", "1-"))
    msgs.start(*both("1++", "1--", "b+", "b-", "c+", "c-"))

    @pl.when(early)
    def _():
        query_copy.wait_recv()
        load_queries(guest, [qbuf[:, i * dh : (i + 1) * dh] for i in range(given)])
        for h in guest:
            top[h] = jnp.full((tok, dh), NEGATIVE, F32)
            tot[h] = jnp.zeros((tok, dh), F32)
            acc[h] = jnp.zeros((tok, dh), F32)
        attend(guest, k4t[me], v4[me])

    def block(j):
        @pl.when(j < me)
        def _():
            keys, values, b, v2 = prepare(j)
            attend(main, keys, values)
            s, c = quad(dot_rows(pair(b), v2)), jnp.sum(b, axis=0, keepdims=True)
            add_state(0, s, c)
            add_state(1, s, c)

            @pl.when(early)
            def _():
                attend(rest + guest, keys, values)

        @pl.when(jnp.logical_and(j > me, j <= far))
        def _():
            keys, values, b, v2 = prepare(j)

            @pl.when(j < far)
            def _():
                attend(guest, keys, values)
                add_state(1, quad(dot_rows(pair(b), v2)), jnp.sum(b, axis=0, keepdims=True))

            @pl.when(j == far)
            def _():
                diagonal(1, b, vbuf[j])
                before(guest, rest, 1, j, False)

    order = (
        (0, 3), (0, 1), (3, 0), (1, 0), (0, 2), (2, 0), (3, 3), (3, 1), (1, 3), (1, 1),
        (3, 2), (1, 2), (2, 3), (2, 1), (2, 2),
    )

    def step(t, _):
        @pl.when(t == 0)
        def _():
            msgs.arrived(*both("a+", "a-"))
            msgs.start(*both("a++", "a--"))

        @pl.when(t == 4)
        def _():
            msgs.arrived(*both("1++", "1--"))
            msgs.start(*both("d+", "d-"))
            msgs.arrived(*both("a++", "a--"))

        @pl.when(t == 6)
        def _():
            msgs.arrived(*both("b+", "b-", "c+", "c-"))
            msgs.start(*both("b++", "b--", "c++", "c--"))

        @pl.when(t == 10)
        def _():
            msgs.arrived(*both("d+", "d-"))
            msgs.start(*both("d++", "d--"))
            msgs.arrived(*both("b++", "b--", "c++", "c--"))

        @pl.when(t == 14)
        def _():
            msgs.arrived(*both("d++", "d--"))

        dx, dz = jnp.int32(0), jnp.int32(0)
        for i, (ox, oz) in enumerate(order):
            dx = jnp.where(t == i, ox, dx)
            dz = jnp.where(t == i, oz, dz)
        block(at(dx, dz))
        return 0

    lax.fori_loop(0, n_seq - 1, step, 0)

    def after(slots, n):
        state2 = twice(pair(state[n]), 0)
        state2t = twice(pair(state[n].T), 0)
        norm_row = norm[n]
        feats = [feat[h] for h in slots]
        a2s = [a4[h, :, : 2 * dh] for h in slots]
        inter = [fold(dot(a2, state2)) for a2 in a2s]
        gns, gds = [], []
        for h, a, more in zip(slots, feats, inter):
            rden = 1.0 / (den[h] + jnp.sum(a * norm_row, axis=1, keepdims=True))
            student = (num[h] + more) * rden
            teacher = acc[h] / jnp.sum(tot[h], axis=1, keepdims=True)
            gn = (student - teacher) * rden
            gns.append(pair(gn))
            gds.append(-jnp.sum(gn * student, axis=1, keepdims=True))
        coups = [dot(twice(gn2, 1), v4t[n]) for gn2 in gns]
        c2s = [pair(jnp.where(causal, c + gd, 0.0)) for c, gd in zip(coups, gds)]
        gqs = [
            fold(dot(c2, b4[n])) + fold(dot(gn2, state2t)) + gd * norm_row
            for c2, gn2, gd in zip(c2s, gns, gds)
        ]
        grads = [quad(dot_rows(q4[h, :, : 2 * dh], pair(g * sgq[h]))) for h, g in zip(slots, gqs)]
        adj = sum(quad(dot_rows(a2, gn2)) for a2, gn2 in zip(a2s, gns))
        adjn = sum(jnp.sum(a * gd, axis=0, keepdims=True) for a, gd in zip(feats, gds))
        gkd = sum(quad(dot_rows(c2, a2)) for c2, a2 in zip(c2s, a2s))
        return grads, adj, adjn, gkd

    width = dh // n_seq
    groups = ((0, cut), (cut, heads - cut), (heads, 1))

    def rows_of(d):
        return pl.ds(pl.multiple_of(d * width, width), width)

    def scatter(g):
        first, count = groups[g]

        def send(k, _):
            peer = lax.rem(me + k, n_seq)
            pltpu.make_async_remote_copy(
                src_ref=grad.at[pl.ds(first, count), rows_of(peer)],
                dst_ref=parts.at[k - 1, pl.ds(first, count)],
                send_sem=rs_send.at[g], recv_sem=rs_recv.at[g],
                device_id={"seq": peer}, device_id_type=MESH,
            ).start()
            return 0

        lax.fori_loop(1, n_seq, send, 0)

    def all_of(ref, sem):
        pltpu.make_async_copy(ref, ref, sem).wait()

    def gather(g):
        first, count = groups[g]
        span = pl.ds(first, count)
        all_of(parts.at[:, span], rs_recv.at[g])
        total = grad[span, rows_of(me)]
        for k in range(n_seq - 1):
            total = total + parts[k, span]
        mine[span] = total
        whole[span, rows_of(me)] = total

        def send(k, _):
            pltpu.make_async_remote_copy(
                src_ref=mine.at[span],
                dst_ref=whole.at[span, rows_of(me)],
                send_sem=ag_send.at[g], recv_sem=ag_recv.at[g],
                device_id={"seq": lax.rem(me + k, n_seq)}, device_id_type=MESH,
            ).start()
            return 0

        lax.fori_loop(1, n_seq, send, 0)
        return jnp.sum(total * total, axis=0)

    def keep(grads, slots):
        for h, g in zip(slots, grads):
            grad[h] = g

    grads, adj, adjn, gkd = after(main[:cut], 0)
    keep(grads, main[:cut])
    scatter(0)
    grads, adj_b, adjn_b, gkd_b = after(main[cut:], 0)
    keep(grads, main[cut:])
    adjs[...] = adj + adj_b
    adjns[0] = adjn + adjn_b
    gkds[0] = gkd + gkd_b

    @pl.when(early)
    def _():
        grads, adj, adjn, gkd = after(rest, 0)
        guests, adj_g, adjn_g, gkd_g = after(guest, 1)
        keep([u + w for u, w in zip(grads, guests)], rest)
        adjs[...] += adj + adj_g
        adjns[0] += adjn + adjn_g
        gkds[0] += gkd
        gkds[1] = gkd_g
        adjt2[1] = twice(pair(adj_g.T), 0)
        adjns[1] = adjn_g

    @pl.when(jnp.logical_not(early))
    def _():
        for h in rest:
            grad[h] = jnp.zeros((dh, dh), F32)

    scatter(1)

    adjt2[0] = twice(pair(adjs[...].T), 0)
    limit = jnp.where(early, far, me)

    def diagonal_grad(n, j):
        return quad(dot(k2t[j], pair(gkds[n] * sgk[j])))

    grad[heads] = diagonal_grad(0, me)

    @pl.when(early)
    def _():
        grad[heads] += diagonal_grad(1, far)

    batch = 4

    def later(c, _):
        js = [batch * c + i for i in range(batch)]
        which = [jnp.where(j < me, 0, 1) for j in js]
        outs = [fold(dot(v4[j, :tok], adjt2[w])) + adjns[w] for j, w in zip(js, which)]
        dks = [pair(jnp.where(j < limit, g * sgk[j], 0.0)) for j, g in zip(js, outs)]
        grad[heads] += quad(sum(dot(k2t[j], dk) for j, dk in zip(js, dks)))
        return 0

    lax.fori_loop(0, (limit + batch - 1) // batch, later, 0)
    scatter(2)
    squares[0] = gather(0) + gather(1)
    squares[0] += gather(2)

    def send_head(k, _):
        pltpu.make_async_remote_copy(
            src_ref=squares.at[0], dst_ref=head_squares.at[k - 1],
            send_sem=sq_send.at[0], recv_sem=sq_recv.at[0],
            device_id={"head": lax.rem(my_head + k, n_head)}, device_id_type=MESH,
        ).start()
        return 0

    def send_seq(k, _):
        pltpu.make_async_remote_copy(
            src_ref=squares.at[1], dst_ref=seq_squares.at[k - 1],
            send_sem=sq_send.at[1], recv_sem=sq_recv.at[1],
            device_id={"seq": lax.rem(me + k, n_seq)}, device_id_type=MESH,
        ).start()
        return 0

    lax.fori_loop(1, n_head, send_head, 0)
    all_of(head_squares, sq_recv.at[0])
    squares[1] = squares[0] + jnp.sum(head_squares[...], axis=0)
    lax.fori_loop(1, n_seq, send_seq, 0)
    all_of(seq_squares, sq_recv.at[1])
    square = jnp.sum(squares[1] + jnp.sum(seq_squares[...], axis=0))
    size = (heads + 1) * n_head * dh * grad.shape[2]
    factor = 1.0 / jnp.sqrt(jnp.broadcast_to(square / size + EPSILON, (1, dh)))
    for g in range(3):
        first, count = groups[g]
        all_of(parts.at[:, pl.ds(first, count)], ag_recv.at[g])
    gq_ref[...] = whole[pl.ds(0, heads)] * factor
    gk_ref[...] = whole[pl.ds(heads, 1)] * factor

    msgs.sent()

    @pl.when(jnp.logical_not(early))
    def _():
        query_copy.wait_send()

    for g in range(3):
        first, count = groups[g]
        all_of(parts.at[:, pl.ds(first, count)], rs_send.at[g])
        all_of(parts.at[:, pl.ds(first, count)], ag_send.at[g])
    all_of(head_squares, sq_send.at[0])
    all_of(seq_squares, sq_send.at[1])


def on_device(queries, key_heads, value_heads, query_map, key_map):
    tok = queries.shape[0]
    heads, dh, feats = query_map.shape
    n = lax.axis_size("seq")
    given = heads // 4
    slots = heads + given
    return pl.pallas_call(
        kernel,
        out_shape=(jax.ShapeDtypeStruct((heads, dh, feats), F32), jax.ShapeDtypeStruct((1, dh, feats), F32)),
        in_specs=[pl.BlockSpec(memory_space=pltpu.VMEM)] * 5,
        out_specs=(pl.BlockSpec(memory_space=pltpu.VMEM),) * 2,
        scratch_shapes=[
            pltpu.VMEM((slots, tok, 4 * dh), BF16),
            pltpu.VMEM((n, 4 * dh, tok), BF16),
            pltpu.VMEM((n, 2 * tok, 2 * dh), BF16),
            pltpu.VMEM((n, 2 * dh, tok), BF16),
            pltpu.VMEM((n, tok, feats), F32),
            pltpu.VMEM((2, feats, dh), F32),
            pltpu.VMEM((2, 1, feats), F32),
        ] + [pltpu.VMEM((slots, tok, dh), F32)] * 6 + [
            pltpu.VMEM((slots, tok, 4 * feats), BF16),
            pltpu.VMEM((slots, tok, feats), F32),
            pltpu.VMEM((2, 2 * tok, 2 * feats), BF16),
            pltpu.VMEM((2, 4 * feats, tok), BF16),
            pltpu.VMEM((2, 4 * dh, tok), BF16),
            pltpu.VMEM((feats, dh), F32),
            pltpu.VMEM((2, 2 * dh, 2 * feats), BF16),
            pltpu.VMEM((2, 1, feats), F32),
            pltpu.VMEM((2, tok, feats), F32),
            pltpu.VMEM((n, tok, dh), F32),
            pltpu.VMEM((n, tok, dh), F32),
            pltpu.VMEM((tok, given * dh), F32),
            pltpu.VMEM((heads + 1, dh, feats), F32),
            pltpu.VMEM((n - 1, heads + 1, dh // n, feats), F32),
            pltpu.VMEM((heads + 1, dh // n, feats), F32),
            pltpu.VMEM((heads + 1, dh, feats), F32),
            pltpu.VMEM((2, dh // n, feats), F32),
            pltpu.VMEM((lax.axis_size("head") - 1, dh // n, feats), F32),
            pltpu.VMEM((n - 1, dh // n, feats), F32),
            pltpu.SemaphoreType.DMA((40,)),
            pltpu.SemaphoreType.DMA((40,)),
            pltpu.SemaphoreType.DMA((1,)),
            pltpu.SemaphoreType.DMA((1,)),
        ] + [pltpu.SemaphoreType.DMA((3,))] * 4 + [pltpu.SemaphoreType.DMA((2,))] * 2,
        compiler_params=pltpu.CompilerParams(vmem_limit_bytes=56 * 2**20, collective_id=0, has_side_effects=True),
    )(queries, key_heads, value_heads, query_map, key_map)


def solution(mesh):
    return jax.shard_map(
        on_device,
        mesh=mesh,
        in_specs=(P("seq", "head"), P("seq", "head"), P("seq", "head"), P("head"), P("head")),
        out_specs=(P("head"), P("head")),
        check_vma=False,
    )
```

time: 98.8 us -> 73 us (0.74)
  Pallas kernels: 95.5 us -> 69.7 us
    pallas_call x1, Pallas kernels: 95.5 us -> 69.7 us  [on_device(): pl.pallas_call(kernel, out_shape=(jax.ShapeDtypeStruct((heads, dh, feats)...]
where the time goes in v1:
time: 73 us; the launch traced here: 72.9 us
  Pallas kernels  69.7 us (95%)
  local copies, waits for them, and re-layouts  2.54 us (3%)
    pallas_call x1, Pallas kernels, on_device(): pl.pallas_call(kernel, out_shape=(jax.ShapeDtypeStruct((heads, dh, feats)...  69.7 us
    unnamed x4, local copies, waits for them, and re-layouts  2.54 us

profile of v1, /device:TPU:1, one launch (start us, length us, event | category | flops | bytes accessed | tf_op | source)
XLA Modules:
  0.0 72.9 jit_solution(16891732830449526073)
XLA Ops:
  0.6 69.7 %shard_map.68 = (f32[8,128,128]{2,1,0:T(8,128)}, f32[1,128,128]{2,1,0:T(8,128)}) custom-call(f32[256,1024]{1,0:T(8,128)} %q_ref.1, f32[256,128]{1,0:T(8,128)} %k_ref.1, f32[256,128]{1,0:T(8,128)} %v_ref.1, f32[8,128,128]{2,1,0:T(8,128)} %qmap_ref.1, f32[1,128,128]{2,1,0:T(8,128)} %kmap_ref.1), custom_call_target="tpu_custom_call" | custom-call | tf_op jit(solution)/shard_map/pallas_call | solution.py:513
  70.3 0.0 copy-start
  70.4 1.9 %copy.9 = f32[8,128,128]{2,1,0:T(8,128)} copy(f32[8,128,128]{2,1,0:T(8,128)} %get-tuple-element.4) | data formatting | bytes 1048576
  72.3 0.0 copy-done
  72.3 0.6 copy.10
Async XLA Ops:
  70.3 1.9 %copy-start = (f32[1,128,128]{2,1,0:T(8,128)S(1)}, f32[1,128,128]{2,1,0:T(8,128)}, u32[]{:S(2)}) copy-start(f32[1,128,128]{2,1,0:T(8,128)} %get-tuple-element.5) | copy-start | bytes 196612

commit v2 on v1

--- a/solution.py
+++ b/solution.py
@@ -234,13 +234,13 @@
     cut = kept // 2
     begin(main[:cut])
     pl.semaphore_wait(barrier, n_head + 4)
-    msgs.start(*both("1+", "1-", "a+", "a-"))
+    msgs.start(*both("1+", "1-"))
+    begin(main[cut:])
+    msgs.start(*both("a+", "a-"))
 
     @pl.when(jnp.logical_not(early))
     def _():
         query_copy.start()
-
-    begin(main[cut:])
 
     @pl.when(early)
     def _():
@@ -249,6 +249,8 @@
 
     msgs.arrived(*both("1+", "1-"))
     msgs.start(*both("1++", "1--", "b+", "b-", "c+", "c-"))
+    msgs.arrived(*both("a+", "a-"))
+    msgs.start(*both("a++", "a--"))
 
     @pl.when(early)
     def _():
@@ -293,11 +295,6 @@
     )
 
     def step(t, _):
-        @pl.when(t == 0)
-        def _():
-            msgs.arrived(*both("a+", "a-"))
-            msgs.start(*both("a++", "a--"))
-
         @pl.when(t == 4)
         def _():
             msgs.arrived(*both("1++", "1--"))
@@ -309,10 +306,13 @@
             msgs.arrived(*both("b+", "b-", "c+", "c-"))
             msgs.start(*both("b++", "b--", "c++", "c--"))
 
-        @pl.when(t == 10)
+        @pl.when(t == 8)
         def _():
             msgs.arrived(*both("d+", "d-"))
             msgs.start(*both("d++", "d--"))
+
+        @pl.when(t == 10)
+        def _():
             msgs.arrived(*both("b++", "b--", "c++", "c--"))
 
         @pl.when(t == 14)
@@ -379,7 +379,7 @@
     def all_of(ref, sem):
         pltpu.make_async_copy(ref, ref, sem).wait()
 
-    def gather(g):
+    def reduce(g):
         first, count = groups[g]
         span = pl.ds(first, count)
         all_of(parts.at[:, span], rs_recv.at[g])
@@ -387,7 +387,11 @@
         for k in range(n_seq - 1):
             total = total + parts[k, span]
         mine[span] = total
-        whole[span, rows_of(me)] = total
+        return jnp.sum(total * total, axis=0)
+
+    def spread(g, first, count):
+        span = pl.ds(first, count)
+        whole[span, rows_of(me)] = mine[span]
 
         def send(k, _):
             pltpu.make_async_remote_copy(
@@ -399,7 +403,6 @@
             return 0
 
         lax.fori_loop(1, n_seq, send, 0)
-        return jnp.sum(total * total, axis=0)
 
     def keep(grads, slots):
         for h, g in zip(slots, grads):
@@ -449,16 +452,19 @@
 
     def later(c, _):
         js = [batch * c + i for i in range(batch)]
+        inside = [j < limit for j in js]
+        js = [jnp.where(ok, j, me) for ok, j in zip(inside, js)]
         which = [jnp.where(j < me, 0, 1) for j in js]
         outs = [fold(dot(v4[j, :tok], adjt2[w])) + adjns[w] for j, w in zip(js, which)]
-        dks = [pair(jnp.where(j < limit, g * sgk[j], 0.0)) for j, g in zip(js, outs)]
+        dks = [pair(jnp.where(ok, g * sgk[j], 0.0)) for ok, j, g in zip(inside, js, outs)]
         grad[heads] += quad(sum(dot(k2t[j], dk) for j, dk in zip(js, dks)))
         return 0
 
     lax.fori_loop(0, (limit + batch - 1) // batch, later, 0)
     scatter(2)
-    squares[0] = gather(0) + gather(1)
-    squares[0] += gather(2)
+    early_squares = reduce(0) + reduce(1)
+    spread(0, 0, heads)
+    squares[0] = early_squares + reduce(2)
 
     def send_head(k, _):
         pltpu.make_async_remote_copy(
@@ -477,6 +483,7 @@
         return 0
 
     lax.fori_loop(1, n_head, send_head, 0)
+    spread(1, heads, 1)
     all_of(head_squares, sq_recv.at[0])
     squares[1] = squares[0] + jnp.sum(head_squares[...], axis=0)
     lax.fori_loop(1, n_seq, send_seq, 0)
@@ -484,9 +491,9 @@
     square = jnp.sum(squares[1] + jnp.sum(seq_squares[...], axis=0))
     size = (heads + 1) * n_head * dh * grad.shape[2]
     factor = 1.0 / jnp.sqrt(jnp.broadcast_to(square / size + EPSILON, (1, dh)))
-    for g in range(3):
-        first, count = groups[g]
-        all_of(parts.at[:, pl.ds(first, count)], ag_recv.at[g])
+    arrived = (parts.at[:, pl.ds(0, heads)], parts.at[:, pl.ds(heads, 1)])
+    for g in range(2):
+        all_of(arrived[g], ag_recv.at[g])
     gq_ref[...] = whole[pl.ds(0, heads)] * factor
     gk_ref[...] = whole[pl.ds(heads, 1)] * factor
 
@@ -499,7 +506,8 @@
     for g in range(3):
         first, count = groups[g]
         all_of(parts.at[:, pl.ds(first, count)], rs_send.at[g])
-        all_of(parts.at[:, pl.ds(first, count)], ag_send.at[g])
+    for g in range(2):
+        all_of(arrived[g], ag_send.at[g])
     all_of(head_squares, sq_send.at[0])
     all_of(seq_squares, sq_send.at[1])
 
@@ -508,7 +516,7 @@
     tok = queries.shape[0]
     heads, dh, feats = query_map.shape
     n = lax.axis_size("seq")
-    given = heads // 4
+    given = heads // 8
     slots = heads + given
     return pl.pallas_call(
         kernel,
@@ -547,7 +555,7 @@
             pltpu.SemaphoreType.DMA((40,)),
             pltpu.SemaphoreType.DMA((1,)),
             pltpu.SemaphoreType.DMA((1,)),
-        ] + [pltpu.SemaphoreType.DMA((3,))] * 4 + [pltpu.SemaphoreType.DMA((2,))] * 2,
+        ] + [pltpu.SemaphoreType.DMA((3,))] * 2 + [pltpu.SemaphoreType.DMA((2,))] * 4,
         compiler_params=pltpu.CompilerParams(vmem_limit_bytes=56 * 2**20, collective_id=0, has_side_effects=True),
     )(queries, key_heads, value_heads, query_map, key_map)
 

time: 73 us -> 69.8 us (0.956)
  Pallas kernels: 69.7 us -> 66.5 us
    pallas_call x1, Pallas kernels: 69.7 us -> 66.5 us  [on_device(): pl.pallas_call(kernel, out_shape=(jax.ShapeDtypeStruct((heads, dh, feats)...]
where the time goes in v2:
time: 69.8 us; the launch traced here: 69.7 us
  Pallas kernels  66.5 us (95%)
  local copies, waits for them, and re-layouts  2.54 us (4%)
    pallas_call x1, Pallas kernels, on_device(): pl.pallas_call(kernel, out_shape=(jax.ShapeDtypeStruct((heads, dh, feats)...  66.5 us
    unnamed x4, local copies, waits for them, and re-layouts  2.54 us

profile of v2, /device:TPU:1, one launch (start us, length us, event | category | flops | bytes accessed | tf_op | source)
XLA Modules:
  0.0 69.7 jit_solution(11114064433959739332)
XLA Ops:
  0.6 66.5 %shard_map.68 = (f32[8,128,128]{2,1,0:T(8,128)}, f32[1,128,128]{2,1,0:T(8,128)}) custom-call(f32[256,1024]{1,0:T(8,128)} %q_ref.1, f32[256,128]{1,0:T(8,128)} %k_ref.1, f32[256,128]{1,0:T(8,128)} %v_ref.1, f32[8,128,128]{2,1,0:T(8,128)} %qmap_ref.1, f32[1,128,128]{2,1,0:T(8,128)} %kmap_ref.1), custom_call_target="tpu_custom_call" | custom-call | tf_op jit(solution)/shard_map/pallas_call | solution.py:521
  67.1 0.0 copy-start
  67.1 1.9 %copy.9 = f32[8,128,128]{2,1,0:T(8,128)} copy(f32[8,128,128]{2,1,0:T(8,128)} %get-tuple-element.4) | data formatting | bytes 1048576
  69.0 0.0 copy-done
  69.0 0.6 copy.10
Async XLA Ops:
  67.1 1.9 %copy-start = (f32[1,128,128]{2,1,0:T(8,128)S(1)}, f32[1,128,128]{2,1,0:T(8,128)}, u32[]{:S(2)}) copy-start(f32[1,128,128]{2,1,0:T(8,128)} %get-tuple-element.5) | copy-start | bytes 196612

commit v3 on v2

--- a/solution.py
+++ b/solution.py
@@ -170,7 +170,7 @@
         v4t[n] = stacked(v.T)
 
     def attend(group, keys, values, masked=False, fresh=False):
-        scores = [dot(q4[h], keys) for h in group]
+        scores = [dot(q4[h, :, : 3 * dh], keys[: 3 * dh]) for h in group]
         if not fresh:
             before = [(top[h], tot[h], acc[h]) for h in group]
         found = []
@@ -184,7 +184,8 @@
                 new = jnp.maximum(before[i][0], new)
                 alpha = jnp.exp2(before[i][0] - new)
             p = jnp.exp2(s - twice(new, 1))
-            o = fold(dot(pair(p), values))
+            hi, lo = halves(p)
+            o = fold(dot(hi, values[:tok]) + dot(lo, values[:tok]))
             t = fold(p)
             if not fresh:
                 t = before[i][1] * alpha + t
@@ -231,7 +232,7 @@
         load_queries(slots, own_queries(slots))
         before(slots, slots, 0, me, True)
 
-    cut = kept // 2
+    cut = (kept + 1) // 2
     begin(main[:cut])
     pl.semaphore_wait(barrier, n_head + 4)
     msgs.start(*both("1+", "1-"))
@@ -448,7 +449,7 @@
     def _():
         grad[heads] += diagonal_grad(1, far)
 
-    batch = 4
+    batch = 8
 
     def later(c, _):
         js = [batch * c + i for i in range(batch)]

time: 69.8 us -> 69.3 us (level)
  no operation moved by 1% of the time
where the time goes in v3:
time: 69.3 us; the launch traced here: 69.2 us
  Pallas kernels  66 us (95%)
  local copies, waits for them, and re-layouts  2.54 us (4%)
    pallas_call x1, Pallas kernels, on_device(): pl.pallas_call(kernel, out_shape=(jax.ShapeDtypeStruct((heads, dh, feats)...  66 us
    unnamed x4, local copies, waits for them, and re-layouts  2.54 us

profile of v3, /device:TPU:1, one launch (start us, length us, event | category | flops | bytes accessed | tf_op | source)
XLA Modules:
  0.0 69.2 jit_solution(10086921076731607475)
XLA Ops:
  0.6 66.0 %shard_map.68 = (f32[8,128,128]{2,1,0:T(8,128)}, f32[1,128,128]{2,1,0:T(8,128)}) custom-call(f32[256,1024]{1,0:T(8,128)} %q_ref.1, f32[256,128]{1,0:T(8,128)} %k_ref.1, f32[256,128]{1,0:T(8,128)} %v_ref.1, f32[8,128,128]{2,1,0:T(8,128)} %qmap_ref.1, f32[1,128,128]{2,1,0:T(8,128)} %kmap_ref.1), custom_call_target="tpu_custom_call" | custom-call | tf_op jit(solution)/shard_map/pallas_call | solution.py:522
  66.6 0.0 copy-start
  66.6 1.9 %copy.9 = f32[8,128,128]{2,1,0:T(8,128)} copy(f32[8,128,128]{2,1,0:T(8,128)} %get-tuple-element.4) | data formatting | bytes 1048576
  68.5 0.0 copy-done
  68.5 0.6 copy.10
Async XLA Ops:
  66.6 1.9 %copy-start = (f32[1,128,128]{2,1,0:T(8,128)S(1)}, f32[1,128,128]{2,1,0:T(8,128)}, u32[]{:S(2)}) copy-start(f32[1,128,128]{2,1,0:T(8,128)} %get-tuple-element.5) | copy-start | bytes 196612

commit v4 on v3

--- a/solution.py
+++ b/solution.py
@@ -249,9 +249,9 @@
         add_state(1, state_own, norm_own)
 
     msgs.arrived(*both("1+", "1-"))
-    msgs.start(*both("1++", "1--", "b+", "b-", "c+", "c-"))
+    msgs.start(*both("1++", "1--", "b+", "b-"))
     msgs.arrived(*both("a+", "a-"))
-    msgs.start(*both("a++", "a--"))
+    msgs.start(*both("a++", "a--", "c+", "c-"))
 
     @pl.when(early)
     def _():
@@ -304,8 +304,13 @@
 
         @pl.when(t == 6)
         def _():
-            msgs.arrived(*both("b+", "b-", "c+", "c-"))
-            msgs.start(*both("b++", "b--", "c++", "c--"))
+            msgs.arrived(*both("b+", "b-"))
+            msgs.start(*both("b++", "b--"))
+
+        @pl.when(t == 7)
+        def _():
+            msgs.arrived(*both("c+", "c-"))
+            msgs.start(*both("c++", "c--"))
 
         @pl.when(t == 8)
         def _():

time: 69.3 us -> 69.1 us (level)
  no operation moved by 1% of the time
where the time goes in v4:
time: 69.1 us; the launch traced here: 68.9 us
  Pallas kernels  65.7 us (95%)
  local copies, waits for them, and re-layouts  2.54 us (4%)
    pallas_call x1, Pallas kernels, on_device(): pl.pallas_call(kernel, out_shape=(jax.ShapeDtypeStruct((heads, dh, feats)...  65.7 us
    unnamed x4, local copies, waits for them, and re-layouts  2.54 us

profile of v4, /device:TPU:1, one launch (start us, length us, event | category | flops | bytes accessed | tf_op | source)
XLA Modules:
  0.0 68.9 jit_solution(16138133868432406504)
XLA Ops:
  0.6 65.7 %shard_map.68 = (f32[8,128,128]{2,1,0:T(8,128)}, f32[1,128,128]{2,1,0:T(8,128)}) custom-call(f32[256,1024]{1,0:T(8,128)} %q_ref.1, f32[256,128]{1,0:T(8,128)} %k_ref.1, f32[256,128]{1,0:T(8,128)} %v_ref.1, f32[8,128,128]{2,1,0:T(8,128)} %qmap_ref.1, f32[1,128,128]{2,1,0:T(8,128)} %kmap_ref.1), custom_call_target="tpu_custom_call" | custom-call | tf_op jit(solution)/shard_map/pallas_call | solution.py:527
  66.4 0.0 copy-start
  66.4 1.9 %copy.9 = f32[8,128,128]{2,1,0:T(8,128)} copy(f32[8,128,128]{2,1,0:T(8,128)} %get-tuple-element.4) | data formatting | bytes 1048576
  68.3 0.0 copy-done
  68.3 0.6 copy.10
Async XLA Ops:
  66.4 1.9 %copy-start = (f32[1,128,128]{2,1,0:T(8,128)S(1)}, f32[1,128,128]{2,1,0:T(8,128)}, u32[]{:S(2)}) copy-start(f32[1,128,128]{2,1,0:T(8,128)} %get-tuple-element.5) | copy-start | bytes 196612

commit v5 on v4

--- a/solution.py
+++ b/solution.py
@@ -251,7 +251,7 @@
     msgs.arrived(*both("1+", "1-"))
     msgs.start(*both("1++", "1--", "b+", "b-"))
     msgs.arrived(*both("a+", "a-"))
-    msgs.start(*both("a++", "a--", "c+", "c-"))
+    msgs.start(*both("a++", "a--"))
 
     @pl.when(early)
     def _():
@@ -296,6 +296,10 @@
     )
 
     def step(t, _):
+        @pl.when(t == 1)
+        def _():
+            msgs.start(*both("c+", "c-"))
+
         @pl.when(t == 4)
         def _():
             msgs.arrived(*both("1++", "1--"))

time: 69.1 us -> 69.3 us (level)
  no operation moved by 1% of the time
where the time goes in v5:
time: 69.3 us; the launch traced here: 69.2 us
  Pallas kernels  66 us (95%)
  local copies, waits for them, and re-layouts  2.54 us (4%)
    pallas_call x1, Pallas kernels, on_device(): pl.pallas_call(kernel, out_shape=(jax.ShapeDtypeStruct((heads, dh, feats)...  66 us
    unnamed x4, local copies, waits for them, and re-layouts  2.54 us

profile of v5, /device:TPU:1, one launch (start us, length us, event | category | flops | bytes accessed | tf_op | source)
XLA Modules:
  0.0 69.2 jit_solution(7495357903943773350)
XLA Ops:
  0.6 66.0 %shard_map.68 = (f32[8,128,128]{2,1,0:T(8,128)}, f32[1,128,128]{2,1,0:T(8,128)}) custom-call(f32[256,1024]{1,0:T(8,128)} %q_ref.1, f32[256,128]{1,0:T(8,128)} %k_ref.1, f32[256,128]{1,0:T(8,128)} %v_ref.1, f32[8,128,128]{2,1,0:T(8,128)} %qmap_ref.1, f32[1,128,128]{2,1,0:T(8,128)} %kmap_ref.1), custom_call_target="tpu_custom_call" | custom-call | tf_op jit(solution)/shard_map/pallas_call | solution.py:531
  66.6 0.0 copy-start
  66.6 1.9 %copy.9 = f32[8,128,128]{2,1,0:T(8,128)} copy(f32[8,128,128]{2,1,0:T(8,128)} %get-tuple-element.4) | data formatting | bytes 1048576
  68.5 0.0 copy-done
  68.5 0.6 copy.10
Async XLA Ops:
  66.6 1.9 %copy-start = (f32[1,128,128]{2,1,0:T(8,128)S(1)}, f32[1,128,128]{2,1,0:T(8,128)}, u32[]{:S(2)}) copy-start(f32[1,128,128]{2,1,0:T(8,128)} %get-tuple-element.5) | copy-start | bytes 196612
